TPU v7x, 32 devices: a whole 2x2x4 slice. The times are simulated.
32 devices in a mesh: dp: 8 (over z, x), mp: 4 (over y, core).
Axes of the slice: x: 2, y: 2, z: 4, core: 2. Of those that a mesh axis runs over, the one named last changes fastest.
Arguments:
- states: bfloat16 [65536, 2048], P(('dp', 'mp')), may hold values from -6 to 6
- dest_device: int32 [65536, 1], P(('dp', 'mp')), may hold values from 0 to 7; in each aligned block of 2048 rows (0 to 2047, 2048 to 4095, ...) at most 320 rows name the same one
- goals: bfloat16 [81920, 1024], P(('dp', 'mp')), may hold values from -6 to 6
- returns: bfloat16 [81920], P(('dp', 'mp')), may hold values from -9 to 9
- weight_in: bfloat16 [3072, 512], P('mp'), may hold values from -0.109375 to 0.109375
- weight_hidden: bfloat16 [3, 512, 512], P(None, 'mp'), may hold values from -0.25 to 0.25
- norm_gain: bfloat16 [4, 512], P(None, 'mp'), may hold values from 0.5 to 1.5
- norm_shift: bfloat16 [4, 512], P(None, 'mp'), may hold values from -1.5 to 1.5
- weight_out: bfloat16 [512], P('mp'), may hold values from -0.25 to 0.25
Outputs:
- total_loss: float32 [], replicated
- grad_states: bfloat16 [65536, 2048], P(('dp', 'mp'))
- grad_goals: bfloat16 [81920, 1024], P(('dp', 'mp'))
- grad_weight_in: float32 [3072, 512], P(None, ('dp', 'mp'))
- grad_weight_hidden: float32 [3, 512, 512], P(None, None, ('dp', 'mp'))
- grad_norm_gain: float32 [4, 512], P(None, ('dp', 'mp'))
- grad_norm_shift: float32 [4, 512], P(None, ('dp', 'mp'))
- grad_weight_out: float32 [512], P(('dp', 'mp'))
Inputs may be any that keep to these rules, and one draw needn't show every extreme that they name: `dest_device`: the 2048 rows of one device name each destination at most 320 times, a bound that some block reaches.
All inputs are finite; a program needn't handle non-finite values.
Results may differ from a plain program's by a relative error of at most 0.019.
Values may be sent and summed in bfloat16 or wider, within the bound.
No kernel may reach another device: no remote copies, remote signals or barrier semaphores. Data moves between devices by JAX's collectives and lax.ppermute only.
A program may use at most 192 MiB of HBM per device.

v0:
```python
import jax
import jax.numpy as jnp
from jax import lax
from jax.sharding import PartitionSpec as P


def norm_act(values, gain, shift):
    center = values - jnp.mean(values, axis=-1, keepdims=True)
    spread = jnp.mean(center * center, axis=-1, keepdims=True)
    return jax.nn.elu(center * lax.rsqrt(spread + 1e-05) * gain + shift)


def left_product(first, second):
    return lax.dot_general(
        first, second, (((0,), (0,)), ((), ())), preferred_element_type=jnp.float32
    )


def right_product(first, second):
    return lax.dot_general(
        first, second, (((1,), (1,)), ((), ())), preferred_element_type=jnp.float32
    )


def shards(
    states, dest_device, goals, returns, weight_in, weight_hidden, norm_gain, norm_shift, weight_out
):
    dp_count = lax.axis_size("dp")
    all_rows = states.shape[0] * dp_count * lax.axis_size("mp")
    slot_count = returns.shape[0]
    capacity = slot_count // dp_count
    feat_width = states.shape[1]
    layer_count = norm_gain.shape[0]
    full_in, full_hidden, full_gain, full_shift, full_out = (
        lax.all_gather(weight_in, "mp", axis=0, tiled=True),
        lax.all_gather(weight_hidden, "mp", axis=1, tiled=True),
        lax.all_gather(norm_gain, "mp", axis=1, tiled=True),
        lax.all_gather(norm_shift, "mp", axis=1, tiled=True),
        lax.all_gather(weight_out, "mp", axis=0, tiled=True),
    )
    dest_index = dest_device[:, 0]
    dest_onehot = (dest_index[:, None] == jnp.arange(dp_count, dtype=jnp.int32)[None, :]).astype(
        jnp.int32
    )
    rank_within = jnp.sum((jnp.cumsum(dest_onehot, axis=0) - dest_onehot) * dest_onehot, axis=1)
    slot_index = dest_index * capacity + rank_within
    send_states = jnp.zeros((slot_count, feat_width), jnp.bfloat16).at[slot_index].set(states)
    send_marks = (
        jnp.zeros((slot_count,), jnp.bfloat16)
        .at[slot_index]
        .set(jnp.ones_like(dest_index, jnp.bfloat16))
    )
    got_states, got_marks = (
        lax.all_to_all(
            send_states.reshape(dp_count, capacity, feat_width),
            "dp",
            split_axis=0,
            concat_axis=0,
            tiled=True,
        ),
        lax.all_to_all(
            send_marks.reshape(dp_count, capacity), "dp", split_axis=0, concat_axis=0, tiled=True
        ),
    )
    row_states = got_states.reshape(slot_count, feat_width)
    valid_mask = got_marks.reshape(slot_count).astype(jnp.float32)
    return_values = returns.astype(jnp.float32)
    local_square = jnp.sum(valid_mask * return_values * return_values)
    square_total = lax.psum(local_square, ("dp", "mp"))
    scale_value = jnp.sqrt(square_total / all_rows + 1e-06)
    inputs = jnp.concatenate([row_states, goals], axis=1)
    layer_inputs = [inputs]
    pullbacks = []
    hidden = inputs
    for layer_number in range(layer_count):
        matrix = full_in if layer_number == 0 else full_hidden[layer_number - 1]
        projected = jnp.dot(hidden, matrix, preferred_element_type=jnp.float32)
        activated, pullback = jax.vjp(
            norm_act,
            projected,
            full_gain[layer_number].astype(jnp.float32),
            full_shift[layer_number].astype(jnp.float32),
        )
        hidden = activated.astype(jnp.bfloat16)
        pullbacks.append(pullback)
        layer_inputs.append(hidden)
    value_pred = jnp.dot(hidden, full_out, preferred_element_type=jnp.float32)
    row_error = valid_mask * (value_pred - return_values / scale_value)
    total_loss = lax.psum(0.5 * jnp.sum(row_error * row_error) / all_rows, ("dp", "mp"))
    grad_value = (row_error / all_rows).astype(jnp.bfloat16)
    grad_out = jnp.dot(grad_value, hidden, preferred_element_type=jnp.float32)
    grad_hidden = grad_value.astype(jnp.float32)[:, None] * full_out.astype(jnp.float32)[None, :]
    hidden_grads = [None] * (layer_count - 1)
    gain_grads = [None] * layer_count
    shift_grads = [None] * layer_count
    grad_in = None
    for layer_number in reversed(range(layer_count)):
        grad_pre, grad_gain, grad_shift = pullbacks[layer_number](grad_hidden)
        grad_pre = grad_pre.astype(jnp.bfloat16)
        gain_grads[layer_number] = grad_gain
        shift_grads[layer_number] = grad_shift
        matrix = full_in if layer_number == 0 else full_hidden[layer_number - 1]
        weight_grad = left_product(layer_inputs[layer_number], grad_pre)
        if layer_number > 0:
            hidden_grads[layer_number - 1] = weight_grad
        else:
            grad_in = weight_grad
        grad_hidden = right_product(grad_pre, matrix)
    grad_state_rows = grad_hidden[:, :feat_width].astype(jnp.bfloat16)
    grad_goal_rows = grad_hidden[:, feat_width:].astype(jnp.bfloat16)
    came_back = lax.all_to_all(
        grad_state_rows.reshape(dp_count, capacity, feat_width),
        "dp",
        split_axis=0,
        concat_axis=0,
        tiled=True,
    )
    grad_states = came_back.reshape(slot_count, feat_width)[slot_index]
    shares = (
        lax.psum_scatter(grad_in, ("dp", "mp"), scatter_dimension=1, tiled=True),
        lax.psum_scatter(jnp.stack(hidden_grads), ("dp", "mp"), scatter_dimension=2, tiled=True),
        lax.psum_scatter(jnp.stack(gain_grads), ("dp", "mp"), scatter_dimension=1, tiled=True),
        lax.psum_scatter(jnp.stack(shift_grads), ("dp", "mp"), scatter_dimension=1, tiled=True),
        lax.psum_scatter(grad_out, ("dp", "mp"), scatter_dimension=0, tiled=True),
    )
    return (
        total_loss,
        grad_states,
        grad_goal_rows,
        shares[0],
        shares[1],
        shares[2],
        shares[3],
        shares[4],
    )


def solution(mesh):
    placed = (
        P(("dp", "mp"), None),
        P(("dp", "mp"), None),
        P(("dp", "mp"), None),
        P(("dp", "mp")),
        P("mp", None),
        P(None, "mp", None),
        P(None, "mp"),
        P(None, "mp"),
        P("mp"),
    )
    return jax.shard_map(
        shards,
        mesh=mesh,
        in_specs=placed,
        out_specs=(
            P(),
            P(("dp", "mp"), None),
            P(("dp", "mp"), None),
            P(None, ("dp", "mp")),
            P(None, None, ("dp", "mp")),
            P(None, ("dp", "mp")),
            P(None, ("dp", "mp")),
            P(("dp", "mp")),
        ),
        check_vma=False,
    )
```

profile of v0, /device:TPU:0, one launch (start us, length us, event | category | flops | bytes accessed | tf_op | source)
XLA Modules:
  0.0 1056.7 jit_solution(1476735436434677186)
XLA Ops:
  7.9 2.3 reduce-window.6
  10.7 0.7 fusion.22
  11.4 0.7 compare_select_fusion.8
  12.2 14.6 %scatter_custom_fusion = bf16[2560]{0:T(1024)(128)(2,1)S(1)} fusion(s32[2048]{0:T(1024)S(1)} %bitcast.104, bf16[2048]{0:T(1024)(128)(2,1)S(1)} %broadcast.175, bf16[]{:T(256)} %constant.61.clone.1), kind=kCustom, calls=%fused_computation.111 | custom fusion | bytes 5122 | tf_op jit(solution)/shard_map/scatter | solution.py:51
  28.7 7.3 all-to-all-start
  36.0 19.2 %scatter_custom_fusion.1 = bf16[2560,2048]{1,0:T(8,128)(2,1)} fusion(s32[2048]{0:T(1024)S(1)} %bitcast.105, bf16[2048,2048]{1,0:T(8,128)(2,1)} %param.9, bf16[]{:T(256)} %constant.61.clone.1), kind=kCustom, calls=%fused_computation.54 | custom fusion | bytes 10486272 | tf_op jit(solution)/shard_map/scatter | solution.py:47
  55.2 6.1 all-to-all-start.1
  62.9 5.0 all-gather
  67.9 5.1 all_gather.16
  73.0 5.1 all_gather.17
  78.9 230.2 %psum.14 = f32[]{:T(128)} all-reduce(f32[]{:T(128)} %fusion.26), channel_id=1, replica_groups=mesh['dp'=8,'mp'=4] {'dp','mp'}, use_global_device_ids=true, to_apply=%region_14.15 | all-reduce | flops 1 | bytes 8 | tf_op jit(solution)/shard_map/psum | solution.py:69
  309.8 14.5 %fusion.48 = (f32[2560]{0:T(1024)S(1)}, f32[2560,512]{0,1:T(8,128)}) fusion(bf16[3072,512]{1,0:T(8,128)(2,1)} %all-gather.4.cloned.1.call-done, bf16[2560,1024]{1,0:T(8,128)(2,1)} %param.11, bf16[2560,2048]{1,0:T(8,128)(2,1)} %bitcast.6), kind=kOutput, calls=%fused_computation.132 | convolution fusion | flops 8085829120 | bytes 24127488 | tf_op jit(solution)/shard_map/dot_general | solution.py:77
  324.4 3.1 multiply_reduce_fusion.11
  327.5 6.2 fusion.49
  334.4 1.9 copy-done.11
  336.3 3.7 fusion.50
  340.6 4.1 fusion.51
  345.4 3.0 fusion.5
  349.4 4.6 fusion.42
  354.0 4.0 fusion.46
  358.0 6.3 multiply_reduce_fusion.1
  364.4 6.5 fusion.45
  370.8 8.6 multiply_reduce_fusion.2
  379.4 4.0 fusion.44
  383.5 4.3 multiply_reduce_fusion.3
  387.8 1.5 fusion.43
  389.4 2.3 copy-done.2
  391.6 13.9 %convolution_convert_fusion = bf16[2560,3072]{1,0:T(8,128)(2,1)} fusion(bf16[3072,512]{1,0:T(8,128)(2,1)} %all-gather.4.cloned.1.call-done, f32[2560,512]{0,1:T(8,128)S(1)} %get-tuple-element.47, f32[2560]{0:T(1024)S(1)} %negate_multiply_fusion), kind=kOutput, calls=%fused_computation.3 | convolution fusion | flops 8063549440 | bytes 24127488 | tf_op jit(solution)/shard_map/dot_general | solution.py:20
  405.6 10.2 slice.79
  415.7 5.3 all-to-all-start.2
  421.1 0.9 copy.45
  422.1 0.9 copy.43
  423.1 7.3 convolution_bitcast_fusion
  430.4 7.3 convolution_bitcast_fusion.1
  437.7 3.1 convolution_bitcast_fusion.2
  440.9 2.0 pad_maximum_fusion.3
  442.8 5.1 copy.38
  448.3 15.0 %fusion = f32[3072,512]{0,1:T(8,128)} fusion(bf16[2560,1024]{1,0:T(8,128)(2,1)} %param.11, bf16[2560,2048]{1,0:T(8,128)(2,1)} %bitcast.6, f32[2560,512]{0,1:T(8,128)} %copy-done.2, f32[2560]{0:T(1024)S(1)} %negate_multiply_fusion), kind=kOutput, calls=%fused_computation.5 | convolution fusion | flops 8087142400 | bytes 27273216 | tf_op jit(solution)/shard_map/dot_general | solution.py:14
  464.6 0.8 fusion.52
  465.4 205.4 %all-reduce.2 = (f32[]{:T(128)}, f32[512]{0:T(512)S(1)}) all-reduce(f32[]{:T(128)S(6)} %div.101, f32[512]{0:T(512)S(1)} %bitcast.116), channel_id=1, replica_groups=mesh['dp'=8,'mp'=4] {'dp','mp'}, use_global_device_ids=true, to_apply=%region_16.17 | all-reduce | flops 513 | bytes 4104 | tf_op jit(solution)/shard_map/psum | solution.py:89
  670.8 5.4 slice.80
  676.8 1.3 copy.46
  678.2 108.3 %reduce-scatter.10.cloned.1.call-done = f32[16,4]{1,0:T(8,128)} async-done(((f32[512,4]{1,0:T(8,128)}), f32[16,4]{1,0:T(8,128)}) %reduce-scatter.10.cloned.1.call-update) | async-done | bytes 272
  786.4 1.3 copy.44
  787.8 142.3 %all-reduce.5.cloned.1.call-done = f32[3,512,512]{1,0,2:T(4,128)} async-done(((f32[3,512,512]{1,0,2:T(4,128)}), f32[3,512,512]{1,0,2:T(4,128)}) %all-reduce.5.cloned.1.call-update) | async-done | bytes 3145744
  930.1 0.9 constant_dynamic-slice_fusion
  931.7 21.6 %gather_fusion = bf16[2048,2048]{1,0:T(8,128)(2,1)} fusion(bf16[2560,2048]{1,0:T(8,128)(2,1)} %bitcast.20, s32[2048]{0:T(1024)S(1)} %broadcast_clamp_fusion), kind=kCustom, calls=%fused_computation | custom fusion | bytes 16785408 | tf_op jit(solution)/shard_map/gather | solution.py:118
  953.3 96.1 %reduce-scatter.8.cloned.1.call-done = f32[3072,16]{0,1:T(8,128)} async-done(((f32[3072,512]{0,1:T(8,128)}), f32[3072,16]{0,1:T(8,128)}) %reduce-scatter.8.cloned.1.call-update) | async-done | bytes 196624 | tf_op jit(solution)/shard_map/reduce_scatter | solution.py:120
  (99 shorter events, 11.2 us)
Async XLA Ops:
  12.2 43.0 %copy-start.5 = (s32[2048,1]{0,1:T(1,128)}, s32[2048,1]{0,1:T(1,128)S(1)}, u32[]{:S(2)}) copy-start(s32[2048,1]{0,1:T(1,128)S(1)} %compare_select_fusion.8) | copy-start | bytes 24580
  28.7 26.4 %all-to-all-start = ((bf16[8,2,160]{2,1,0:T(2,128)(2,1)}), bf16[8,2,160]{2,1,0:T(2,128)(2,1)S(1)}, u32[]{:S(2)}, u32[]{:S(2)}) async-start(bf16[8,2,160]{2,1,0:T(2,128)(2,1)} %reshape.256), calls=%async_computation | async-start | bytes 16384 | tf_op jit(solution)/shard_map/all_to_all | solution.py:61
  55.2 7.7 copy-start.10
  55.2 12.7 %copy-start.8 = (bf16[4,128]{1,0:T(4,128)(2,1)S(1)}, bf16[4,128]{1,0:T(4,128)(2,1)}, u32[]{:S(2)}) copy-start(bf16[4,128]{1,0:T(4,128)(2,1)} %param.15) | copy-start | bytes 3076
  55.2 17.8 %copy-start.9 = (bf16[4,128]{1,0:T(4,128)(2,1)S(1)}, bf16[4,128]{1,0:T(4,128)(2,1)}, u32[]{:S(2)}) copy-start(bf16[4,128]{1,0:T(4,128)(2,1)} %param.16) | copy-start | bytes 3076
  55.2 23.1 %copy-start.7 = (bf16[2560]{0:T(1024)(128)(2,1)S(1)}, bf16[2560]{0:T(1024)(128)(2,1)}, u32[]{:S(2)}) copy-start(bf16[2560]{0:T(1024)(128)(2,1)} %param.12) | copy-start | bytes 15364
  55.2 254.6 %all-to-all-start.1 = ((bf16[8,320,2048]{2,1,0:T(8,128)(2,1)}), bf16[8,320,2048]{2,1,0:T(8,128)(2,1)}, u32[]{:S(2)}, u32[]{:S(2)}) async-start(bf16[8,320,2048]{2,1,0:T(8,128)(2,1)} %bitcast.92), calls=%async_computation.1 | async-start | bytes 20971520 | tf_op jit(solution)/shard_map/all_to_all | solution.py:54
  61.4 248.5 %all-gather.4.cloned.1.call-start = ((), (), s32[]{:S(2)}) async-start(), calls=%async_computation.6 | async-start | bytes 3932160 | tf_op jit(solution)/shard_map/all_gather | solution.py:35
  62.1 265.4 %all-gather.6.cloned.1.call-start = ((), (), s32[]{:S(2)}) async-start(), calls=%async_computation.7 | async-start | bytes 1966080 | tf_op jit(solution)/shard_map/all_gather | solution.py:36
  333.7 45.8 %copy-start = (f32[2560,512]{0,1:T(8,128)}, f32[2560,512]{0,1:T(8,128)S(1)}, u32[]{:S(2)}) copy-start(f32[2560,512]{0,1:T(8,128)S(1)} %get-tuple-element.68) | copy-start | bytes 15728644
  333.7 2.6 copy-start.11
  339.9 24.4 %copy-start.1 = (f32[2560,512]{0,1:T(8,128)}, f32[2560,512]{0,1:T(8,128)S(1)}, u32[]{:S(2)}) copy-start(f32[2560,512]{0,1:T(8,128)S(1)} %get-tuple-element.70) | copy-start | bytes 15728644
  358.0 6.3 copy-start.4
  364.3 19.1 %slice-start = ((s8[5242880]{0:T(1024)(128)(4,1)}), s8[4194304]{0:T(1024)(128)(4,1)S(1)}, s32[]{:S(2)}) async-start(s8[5242880]{0:T(1024)(128)(4,1)} %bitcast.93), calls=%async_computation.12 | async-start | bytes 8388608
  370.8 12.6 %slice-start.1 = ((s8[5242880]{0:T(1024)(128)(4,1)}), s8[1048576]{0:T(1024)(128)(4,1)S(1)}, s32[]{:S(2)}) async-start(s8[5242880]{0:T(1024)(128)(4,1)} %bitcast.93), calls=%async_computation.13 | async-start | bytes 2097152
  383.4 4.4 copy-start.3
  389.3 2.3 copy-start.2
  415.7 516.0 %all-to-all-start.2 = ((bf16[8,320,2048]{2,1,0:T(8,128)(2,1)}), bf16[8,320,2048]{2,1,0:T(8,128)(2,1)}, u32[]{:S(2)}, u32[]{:S(2)}) async-start(bf16[8,320,2048]{2,1,0:T(8,128)(2,1)} %bitcast.91), calls=%async_computation.2 | async-start | bytes 20971520 | tf_op jit(solution)/shard_map/all_to_all | solution.py:111
  421.1 255.8 %reduce-scatter.12.cloned.1.call-start = ((), (), s32[]{:S(2)}) async-start(), calls=%async_computation.10 | async-start | bytes 270336
  422.0 364.4 %reduce-scatter.10.cloned.1.call-start = ((), (), s32[]{:S(2)}) async-start(), calls=%async_computation.9 | async-start | bytes 270336
  423.0 507.1 %all-reduce.5.cloned.1.call-start = ((), (), s32[]{:S(2)}) async-start(), calls=%async_computation.11 | async-start | bytes 8388608
  423.1 14.6 %slice-start.2 = ((s8[5242880]{0:T(1024)(128)(4,1)}), s8[4194304]{0:T(1024)(128)(4,1)S(1)}, s32[]{:S(2)}) async-start(s8[5242880]{0:T(1024)(128)(4,1)} %bitcast.95), calls=%async_computation.14 | async-start | bytes 8388608
  423.1 14.6 %slice-start.4 = ((s8[5242880]{0:T(1024)(128)(4,1)}), s8[4194304]{0:T(1024)(128)(4,1)S(1)}, s32[]{:S(2)}) async-start(s8[5242880]{0:T(1024)(128)(4,1)} %bitcast.97), calls=%async_computation.16 | async-start | bytes 8388608
  430.4 7.3 slice-start.3
  430.4 7.3 slice-start.5
  448.0 601.4 %reduce-scatter.8.cloned.1.call-start = ((), (), s32[]{:S(2)}) async-start(), calls=%async_computation.8 | async-start | bytes 6488064 | tf_op jit(solution)/shard_map/reduce_scatter | solution.py:120
  463.3 0.7 copy-start.6
Sparse Core Ops, SparseCore 0:
  63.8 30.3 all-gather.3
  95.7 19.6 all-gather.5
  424.1 226.0 reduce-scatter.11
  652.4 133.9 reduce-scatter.9
  792.4 137.6 all-reduce.4
  936.1 113.2 reduce-scatter.7
where the time goes:
time: 1060 us
  blocking collectives  451 us (43%)
  waiting for transfers between devices  348 us (33%)
  matrix products  95.5 us (9%)
  local copies, waits for them, and re-layouts  89.3 us (8%)
  other arithmetic  37.3 us (4%)
  starting transfers between devices  19.2 us (2%)
  between operations  16.4 us (2%)
    unnamed x9, waiting for transfers between devices  252 us
    psum x1, blocking collectives, shards(): square_total = lax.psum(local_square, ('dp', 'mp'))  230 us
    psum x1, blocking collectives, shards(): lax.psum(0.5 * jnp.sum(row_error * row_error) / all_rows, ('dp', 'mp'))  205 us
    reduce_scatter x1, waiting for transfers between devices, shards(): lax.psum_scatter(grad_in, ('dp', 'mp'), scatter_dimension=1, tiled=True)  96.1 us
    dot_general x4, matrix products, right_product(): lax.dot_general(first, second, (((1,), (1,)), ((), ())), preferred_elemen...  33.1 us
    dot_general x4, matrix products, left_product(): lax.dot_general(first, second, (((0,), (0,)), ((), ())), preferred_elemen...  32.8 us
    dot_general x4, matrix products, shards(): projected = jnp.dot(hidden, matrix, preferred_element_type=jnp.float32)  28.5 us
    gather x1, local copies, waits for them, and re-layouts, shards(): grad_states = came_back.reshape(slot_count, feat_width)[slot_index]  21.6 us
  transfers between devices with their start and end apart: 9, of which 3 were waited for; matrix products, arithmetic and copies ran while one was open for 11% of the time, Pallas kernels for 0%

commit v1 on v0

--- a/solution.py
+++ b/solution.py
@@ -86,7 +86,7 @@
         layer_inputs.append(hidden)
     value_pred = jnp.dot(hidden, full_out, preferred_element_type=jnp.float32)
     row_error = valid_mask * (value_pred - return_values / scale_value)
-    total_loss = lax.psum(0.5 * jnp.sum(row_error * row_error) / all_rows, ("dp", "mp"))
+    total_loss = lax.psum(lax.psum(0.5 * jnp.sum(row_error * row_error) / all_rows, "dp"), "mp")
     grad_value = (row_error / all_rows).astype(jnp.bfloat16)
     grad_out = jnp.dot(grad_value, hidden, preferred_element_type=jnp.float32)
     grad_hidden = grad_value.astype(jnp.float32)[:, None] * full_out.astype(jnp.float32)[None, :]

time: 1060 us -> 1070 us (level)
  blocking collectives: 451 us -> 486 us
  waiting for transfers between devices: 348 us -> 316 us
    unnamed x0 -> x1, blocking collectives: none -> 72.4 us
    psum x1 -> x2, blocking collectives: 205 us -> 168 us  [the longest x1 142 us: shards(): lax.psum(0.5 * jnp.sum(row_error * row_error) / all_rows, 'dp')]
    unnamed x9, waiting for transfers between devices: 252 us -> 220 us
where the time goes in v1:
time: 1070 us; the launch traced here: 1060 us
  blocking collectives  486 us (45%)
  waiting for transfers between devices  316 us (30%)
  matrix products  95.5 us (9%)
  local copies, waits for them, and re-layouts  89.3 us (8%)
  other arithmetic  37.3 us (3%)
  starting transfers between devices  19.2 us (2%)
  between operations  16.4 us (2%)
    psum x1, blocking collectives, shards(): square_total = lax.psum(local_square, ('dp', 'mp'))  230 us
    unnamed x9, waiting for transfers between devices  220 us
    psum x1, blocking collectives, shards(): lax.psum(0.5 * jnp.sum(row_error * row_error) / all_rows, 'dp')  142 us
    reduce_scatter x1, waiting for transfers between devices, shards(): lax.psum_scatter(grad_in, ('dp', 'mp'), scatter_dimension=1, tiled=True)  96.1 us
    unnamed x1, blocking collectives  72.4 us
    dot_general x4, matrix products, right_product(): lax.dot_general(first, second, (((1,), (1,)), ((), ())), preferred_elemen...  33.1 us
    dot_general x4, matrix products, left_product(): lax.dot_general(first, second, (((0,), (0,)), ((), ())), preferred_elemen...  32.8 us
    dot_general x4, matrix products, shards(): projected = jnp.dot(hidden, matrix, preferred_element_type=jnp.float32)  28.5 us
  transfers between devices with their start and end apart: 9, of which 3 were waited for; matrix products, arithmetic and copies ran while one was open for 11% of the time, Pallas kernels for 0%

profile of v1, /device:TPU:0, one launch (start us, length us, event | category | flops | bytes accessed | tf_op | source)
XLA Modules:
  0.0 1059.7 jit_solution(16021899390404381443)
XLA Ops:
  7.9 2.3 reduce-window.6
  12.2 14.6 %scatter_custom_fusion = bf16[2560]{0:T(1024)(128)(2,1)S(1)} fusion(s32[2048]{0:T(1024)S(1)} %bitcast.104, bf16[2048]{0:T(1024)(128)(2,1)S(1)} %broadcast.175, bf16[]{:T(256)} %constant.61.clone.1), kind=kCustom, calls=%fused_computation.111 | custom fusion | bytes 5122 | tf_op jit(solution)/shard_map/scatter | solution.py:51
  28.7 7.3 all-to-all-start
  36.0 19.2 %scatter_custom_fusion.1 = bf16[2560,2048]{1,0:T(8,128)(2,1)} fusion(s32[2048]{0:T(1024)S(1)} %bitcast.105, bf16[2048,2048]{1,0:T(8,128)(2,1)} %param.9, bf16[]{:T(256)} %constant.61.clone.1), kind=kCustom, calls=%fused_computation.54 | custom fusion | bytes 10486272 | tf_op jit(solution)/shard_map/scatter | solution.py:47
  55.2 6.1 all-to-all-start.1
  62.9 5.0 all-gather
  67.9 5.1 all_gather.16
  73.0 5.1 all_gather.17
  78.9 230.2 %psum.21 = f32[]{:T(128)} all-reduce(f32[]{:T(128)} %fusion.26), channel_id=1, replica_groups=mesh['dp'=8,'mp'=4] {'dp','mp'}, use_global_device_ids=true, to_apply=%region_14.15 | all-reduce | flops 1 | bytes 8 | tf_op jit(solution)/shard_map/psum | solution.py:69
  309.8 14.5 %fusion.48 = (f32[2560]{0:T(1024)S(1)}, f32[2560,512]{0,1:T(8,128)}) fusion(bf16[3072,512]{1,0:T(8,128)(2,1)} %all-gather.4.cloned.1.call-done, bf16[2560,1024]{1,0:T(8,128)(2,1)} %param.11, bf16[2560,2048]{1,0:T(8,128)(2,1)} %bitcast.6), kind=kOutput, calls=%fused_computation.132 | convolution fusion | flops 8085829120 | bytes 24127488 | tf_op jit(solution)/shard_map/dot_general | solution.py:77
  324.4 3.1 multiply_reduce_fusion.11
  327.5 6.2 fusion.49
  334.4 1.9 copy-done.11
  336.3 3.7 fusion.50
  340.6 4.1 fusion.51
  345.4 3.0 fusion.5
  349.4 4.6 fusion.42
  354.0 4.0 fusion.46
  358.0 6.3 multiply_reduce_fusion.1
  364.4 6.5 fusion.45
  370.8 8.6 multiply_reduce_fusion.2
  379.4 4.0 fusion.44
  383.5 4.3 multiply_reduce_fusion.3
  387.8 1.5 fusion.43
  389.4 2.3 copy-done.2
  391.6 13.9 %convolution_convert_fusion = bf16[2560,3072]{1,0:T(8,128)(2,1)} fusion(bf16[3072,512]{1,0:T(8,128)(2,1)} %all-gather.4.cloned.1.call-done, f32[2560,512]{0,1:T(8,128)S(1)} %get-tuple-element.45, f32[2560]{0:T(1024)S(1)} %negate_multiply_fusion), kind=kOutput, calls=%fused_computation.3 | convolution fusion | flops 8063549440 | bytes 24127488 | tf_op jit(solution)/shard_map/dot_general | solution.py:20
  405.6 10.2 slice.79
  415.7 5.3 all-to-all-start.2
  421.1 0.9 copy.45
  422.1 0.9 copy.43
  423.1 7.3 convolution_bitcast_fusion
  430.4 7.3 convolution_bitcast_fusion.1
  437.7 3.1 convolution_bitcast_fusion.2
  440.9 2.0 pad_maximum_fusion.3
  442.8 5.1 copy.38
  448.3 15.0 %fusion = f32[3072,512]{0,1:T(8,128)} fusion(bf16[2560,1024]{1,0:T(8,128)(2,1)} %param.11, bf16[2560,2048]{1,0:T(8,128)(2,1)} %bitcast.6, f32[2560,512]{0,1:T(8,128)} %copy-done.2, f32[2560]{0:T(1024)S(1)} %negate_multiply_fusion), kind=kOutput, calls=%fused_computation.5 | convolution fusion | flops 8087142400 | bytes 27273216 | tf_op jit(solution)/shard_map/dot_general | solution.py:14
  464.6 141.9 %psum.22 = f32[]{:T(128)} all-reduce(f32[]{:T(128)S(6)} %div.101), channel_id=1, replica_groups=mesh['dp'=8,'mp'=4] {'dp'}, use_global_device_ids=true, to_apply=%region_16.17 | all-reduce | flops 1 | bytes 8 | tf_op jit(solution)/shard_map/psum | solution.py:89
  606.5 26.1 %psum.23 = f32[]{:T(128)} all-reduce(f32[]{:T(128)} %psum.22), channel_id=1, replica_groups=mesh['dp'=8,'mp'=4] {'mp'}, use_global_device_ids=true, to_apply=%region_17.18 | all-reduce | flops 1 | bytes 8 | tf_op jit(solution)/shard_map/psum | solution.py:89
  632.6 5.4 slice.80
  638.0 0.8 fusion.52
  638.8 72.4 %all-reduce.1 = f32[512]{0:T(512)S(1)} all-reduce(f32[512]{0:T(512)S(1)} %bitcast.116), channel_id=6, replica_groups=mesh['dp'=8,'mp'=4] {'dp','mp'}, use_global_device_ids=true, to_apply=%region_38.39.clone | all-reduce | flops 512 | bytes 4096
  711.8 1.3 copy.46
  713.2 76.3 %reduce-scatter.10.cloned.1.call-done = f32[16,4]{1,0:T(8,128)} async-done(((f32[512,4]{1,0:T(8,128)}), f32[16,4]{1,0:T(8,128)}) %reduce-scatter.10.cloned.1.call-update) | async-done | bytes 272
  789.5 1.3 copy.44
  790.9 142.3 %all-reduce.4.cloned.1.call-done = f32[3,512,512]{1,0,2:T(4,128)} async-done(((f32[3,512,512]{1,0,2:T(4,128)}), f32[3,512,512]{1,0,2:T(4,128)}) %all-reduce.4.cloned.1.call-update) | async-done | bytes 3145744
  933.1 0.9 constant_dynamic-slice_fusion
  934.7 21.6 %gather_fusion = bf16[2048,2048]{1,0:T(8,128)(2,1)} fusion(bf16[2560,2048]{1,0:T(8,128)(2,1)} %bitcast.20, s32[2048]{0:T(1024)S(1)} %broadcast_clamp_fusion), kind=kCustom, calls=%fused_computation | custom fusion | bytes 16785408 | tf_op jit(solution)/shard_map/gather | solution.py:118
  956.4 96.1 %reduce-scatter.8.cloned.1.call-done = f32[3072,16]{0,1:T(8,128)} async-done(((f32[3072,512]{0,1:T(8,128)}), f32[3072,16]{0,1:T(8,128)}) %reduce-scatter.8.cloned.1.call-update) | async-done | bytes 196624 | tf_op jit(solution)/shard_map/reduce_scatter | solution.py:120
  (101 shorter events, 12.7 us)
Async XLA Ops:
  12.2 43.0 %copy-start.5 = (s32[2048,1]{0,1:T(1,128)}, s32[2048,1]{0,1:T(1,128)S(1)}, u32[]{:S(2)}) copy-start(s32[2048,1]{0,1:T(1,128)S(1)} %compare_select_fusion.8) | copy-start | bytes 24580
  28.7 26.4 %all-to-all-start = ((bf16[8,2,160]{2,1,0:T(2,128)(2,1)}), bf16[8,2,160]{2,1,0:T(2,128)(2,1)S(1)}, u32[]{:S(2)}, u32[]{:S(2)}) async-start(bf16[8,2,160]{2,1,0:T(2,128)(2,1)} %reshape.256), calls=%async_computation | async-start | bytes 16384 | tf_op jit(solution)/shard_map/all_to_all | solution.py:61
  55.2 7.7 copy-start.10
  55.2 12.7 %copy-start.8 = (bf16[4,128]{1,0:T(4,128)(2,1)S(1)}, bf16[4,128]{1,0:T(4,128)(2,1)}, u32[]{:S(2)}) copy-start(bf16[4,128]{1,0:T(4,128)(2,1)} %param.15) | copy-start | bytes 3076
  55.2 17.8 %copy-start.9 = (bf16[4,128]{1,0:T(4,128)(2,1)S(1)}, bf16[4,128]{1,0:T(4,128)(2,1)}, u32[]{:S(2)}) copy-start(bf16[4,128]{1,0:T(4,128)(2,1)} %param.16) | copy-start | bytes 3076
  55.2 23.1 %copy-start.7 = (bf16[2560]{0:T(1024)(128)(2,1)S(1)}, bf16[2560]{0:T(1024)(128)(2,1)}, u32[]{:S(2)}) copy-start(bf16[2560]{0:T(1024)(128)(2,1)} %param.12) | copy-start | bytes 15364
  55.2 254.6 %all-to-all-start.1 = ((bf16[8,320,2048]{2,1,0:T(8,128)(2,1)}), bf16[8,320,2048]{2,1,0:T(8,128)(2,1)}, u32[]{:S(2)}, u32[]{:S(2)}) async-start(bf16[8,320,2048]{2,1,0:T(8,128)(2,1)} %bitcast.92), calls=%async_computation.1 | async-start | bytes 20971520 | tf_op jit(solution)/shard_map/all_to_all | solution.py:54
  61.4 248.5 %all-gather.4.cloned.1.call-start = ((), (), s32[]{:S(2)}) async-start(), calls=%async_computation.6 | async-start | bytes 3932160 | tf_op jit(solution)/shard_map/all_gather | solution.py:35
  62.1 265.4 %all-gather.6.cloned.1.call-start = ((), (), s32[]{:S(2)}) async-start(), calls=%async_computation.7 | async-start | bytes 1966080 | tf_op jit(solution)/shard_map/all_gather | solution.py:36
  333.7 45.8 %copy-start = (f32[2560,512]{0,1:T(8,128)}, f32[2560,512]{0,1:T(8,128)S(1)}, u32[]{:S(2)}) copy-start(f32[2560,512]{0,1:T(8,128)S(1)} %get-tuple-element.66) | copy-start | bytes 15728644
  333.7 2.6 copy-start.11
  339.9 24.4 %copy-start.1 = (f32[2560,512]{0,1:T(8,128)}, f32[2560,512]{0,1:T(8,128)S(1)}, u32[]{:S(2)}) copy-start(f32[2560,512]{0,1:T(8,128)S(1)} %get-tuple-element.68) | copy-start | bytes 15728644
  358.0 6.3 copy-start.4
  364.3 19.1 %slice-start = ((s8[5242880]{0:T(1024)(128)(4,1)}), s8[4194304]{0:T(1024)(128)(4,1)S(1)}, s32[]{:S(2)}) async-start(s8[5242880]{0:T(1024)(128)(4,1)} %bitcast.93), calls=%async_computation.12 | async-start | bytes 8388608
  370.8 12.6 %slice-start.1 = ((s8[5242880]{0:T(1024)(128)(4,1)}), s8[1048576]{0:T(1024)(128)(4,1)S(1)}, s32[]{:S(2)}) async-start(s8[5242880]{0:T(1024)(128)(4,1)} %bitcast.93), calls=%async_computation.13 | async-start | bytes 2097152
  383.4 4.4 copy-start.3
  389.3 2.3 copy-start.2
  415.7 519.0 %all-to-all-start.2 = ((bf16[8,320,2048]{2,1,0:T(8,128)(2,1)}), bf16[8,320,2048]{2,1,0:T(8,128)(2,1)}, u32[]{:S(2)}, u32[]{:S(2)}) async-start(bf16[8,320,2048]{2,1,0:T(8,128)(2,1)} %bitcast.91), calls=%async_computation.2 | async-start | bytes 20971520 | tf_op jit(solution)/shard_map/all_to_all | solution.py:111
  421.1 290.8 %reduce-scatter.12.cloned.1.call-start = ((), (), s32[]{:S(2)}) async-start(), calls=%async_computation.10 | async-start | bytes 270336
  422.0 367.5 %reduce-scatter.10.cloned.1.call-start = ((), (), s32[]{:S(2)}) async-start(), calls=%async_computation.9 | async-start | bytes 270336
  423.0 510.1 %all-reduce.4.cloned.1.call-start = ((), (), s32[]{:S(2)}) async-start(), calls=%async_computation.11 | async-start | bytes 8388608
  423.1 14.6 %slice-start.2 = ((s8[5242880]{0:T(1024)(128)(4,1)}), s8[4194304]{0:T(1024)(128)(4,1)S(1)}, s32[]{:S(2)}) async-start(s8[5242880]{0:T(1024)(128)(4,1)} %bitcast.95), calls=%async_computation.14 | async-start | bytes 8388608
  423.1 14.6 %slice-start.4 = ((s8[5242880]{0:T(1024)(128)(4,1)}), s8[4194304]{0:T(1024)(128)(4,1)S(1)}, s32[]{:S(2)}) async-start(s8[5242880]{0:T(1024)(128)(4,1)} %bitcast.97), calls=%async_computation.16 | async-start | bytes 8388608
  430.4 7.3 slice-start.3
  430.4 7.3 slice-start.5
  448.0 604.5 %reduce-scatter.8.cloned.1.call-start = ((), (), s32[]{:S(2)}) async-start(), calls=%async_computation.8 | async-start | bytes 6488064 | tf_op jit(solution)/shard_map/reduce_scatter | solution.py:120
  463.3 0.7 copy-start.6
Sparse Core Ops, SparseCore 0:
  63.8 30.3 all-gather.3
  95.7 19.6 all-gather.5
  424.1 232.6 reduce-scatter.11
  659.0 130.5 reduce-scatter.9
  795.5 137.6 all-reduce.3
  939.2 113.2 reduce-scatter.7
